TPU v7x, 512 devices: a whole 4x4x16 slice. The times are simulated.
512 devices in a mesh: dp: 4 (over y), row: 4 (over x), col: 32 (over z, core).
Axes of the slice: x: 4, y: 4, z: 16, core: 2. Of those that a mesh axis runs over, the one named last changes fastest.
Arguments:
- inputs: bfloat16 [2048, 6144], P(('dp', 'row'), 'col'), may hold values from -6 to 6
- out_grad: bfloat16 [2048, 6144], P(('dp', 'row'), 'col'), may hold values from -6 to 6
- up_blocks: bfloat16 [4, 32, 16, 128, 128], P('row', 'col'), may hold values from -0.25 to 0.25
- up_index: int32 [4, 32, 16], P('row', 'col'), may hold values from -1 to 71, as said below
- down_blocks: bfloat16 [4, 32, 16, 128, 128], P('row', 'col'), may hold values from -0.125 to 0.125
- down_index: int32 [4, 32, 16], P('row', 'col'), may hold values from -1 to 71, as said below
Outputs:
- in_grad: bfloat16 [2048, 6144], P(('dp', 'row'), 'col')
- up_grad: bfloat16 [4, 32, 16, 128, 128], P('row', 'col', 'dp')
- down_grad: bfloat16 [4, 32, 16, 128, 128], P('row', 'col', 'dp')
Inputs may be any that keep to these rules, and one draw needn't show every extreme that they name: `up_index`: in each shard the indices of the first slots are distinct positions of 0 to 71 and all later slots are -1. Some shard fills all 16 slots; the shards of one column slab together hold at most 46 kept blocks, and some column slab holds exactly 46. `down_index`: as for up_index, with positions of 0 to 71; some shard fills all 16 slots and some column slab holds exactly 46 kept blocks.
All inputs are finite; a program needn't handle non-finite values.
Results may differ from a plain program's by a relative error of at most 0.022.
Values may be sent and summed in bfloat16 or wider, within the bound.
A program may use at most 64 MiB of HBM per device.

v0:
```python
import math

import jax
import jax.numpy as jnp
from jax import lax
from jax.sharding import PartitionSpec as P

H = 24576


root_two_pi = math.sqrt(2.0 / math.pi)


def gelu_parts(value):
    inner = root_two_pi * (value + 0.044715 * value * value * value)
    tanh_inner = jnp.tanh(inner)
    result = 0.5 * value * (1.0 + tanh_inner)
    slope = 0.5 * (1.0 + tanh_inner) + 0.5 * value * (
        1.0 - tanh_inner * tanh_inner
    ) * root_two_pi * (1.0 + 3.0 * 0.044715 * value * value)
    return (result, slope)


def slot_lists(blocks, index):
    owners_count = blocks.shape[0]
    slots_each = blocks.shape[2]
    side = blocks.shape[-1]
    total = owners_count * slots_each
    flat_blocks = blocks.reshape(total, side, side)
    flat_index = index.reshape(total)
    owner = jnp.arange(total, dtype=jnp.int32) // slots_each
    valid = flat_index >= 0
    flat_blocks = flat_blocks * valid.astype(jnp.bfloat16)[:, None, None]
    position = jnp.maximum(flat_index, 0)
    return (flat_blocks, position, owner, valid)


def onehot_rows(labels, width):
    return (labels[:, None] == jnp.arange(width, dtype=jnp.int32)[None, :]).astype(jnp.float32)


def body(inputs, out_grad, up_blocks, up_index, down_blocks, down_index):
    highest = lax.Precision.HIGHEST
    row_count = lax.axis_size("row")
    col_count = lax.axis_size("col")
    replicas = lax.axis_size("dp")
    tokens_here = inputs.shape[0]
    width = inputs.shape[1] * col_count
    side = up_blocks.shape[-1]
    per_row = width // (side * row_count)
    per_slab = H // (side * col_count)
    block_rows = width // side
    scale = 1.0 / math.sqrt(tokens_here * row_count * replicas)
    input_full, cotan_full = (
        lax.all_gather(inputs, "col", axis=1, tiled=True),
        lax.all_gather(out_grad, "col", axis=1, tiled=True),
    )
    up_gathered, up_listing = (
        lax.all_gather(up_blocks, "row", axis=0, tiled=True),
        lax.all_gather(up_index, "row", axis=0, tiled=True),
    )
    up_matrix, up_place, up_owner, up_valid = slot_lists(up_gathered, up_listing)
    up_row = up_owner * per_row + up_place // per_slab
    up_col = up_place % per_slab
    input_tiles = input_full.reshape(tokens_here, block_rows, side)
    input_taken = jnp.take(input_tiles, up_row, axis=1)
    product = jnp.einsum("tsk,skn->tsn", input_taken, up_matrix, preferred_element_type=jnp.float32)
    pre_act = jnp.einsum("tsn,sc->tcn", product, onehot_rows(up_col, per_slab), precision=highest)
    act_value, slope = gelu_parts(pre_act)
    act_low = act_value.astype(jnp.bfloat16)
    up_gathered, up_listing, down_gathered, down_listing = (
        lax.all_gather(up_blocks, "row", axis=0, tiled=True),
        lax.all_gather(up_index, "row", axis=0, tiled=True),
        lax.all_gather(down_blocks, "row", axis=0, tiled=True),
        lax.all_gather(down_index, "row", axis=0, tiled=True),
    )
    up_matrix, up_place, up_owner, up_valid = slot_lists(up_gathered, up_listing)
    up_row = up_owner * per_row + up_place // per_slab
    up_col = up_place % per_slab
    down_matrix, down_place, down_owner, down_valid = slot_lists(down_gathered, down_listing)
    down_row = down_place // per_row
    down_col = down_owner * per_row + down_place % per_row
    cotan_tiles = cotan_full.reshape(tokens_here, block_rows, side)
    cotan_taken = jnp.take(cotan_tiles, down_col, axis=1)
    act_terms = jnp.einsum(
        "tsj,sij->tsi", cotan_taken, down_matrix, preferred_element_type=jnp.float32
    )
    act_grad = jnp.einsum(
        "tsi,sc->tci", act_terms, onehot_rows(down_row, per_slab), precision=highest
    )
    pre_grad = (act_grad * slope).astype(jnp.bfloat16)
    pre_taken = jnp.take(pre_grad, up_col, axis=1)
    input_terms = jnp.einsum(
        "tsn,skn->tsk", pre_taken, up_matrix, preferred_element_type=jnp.float32
    )
    input_slab = jnp.einsum(
        "tsk,sb->tbk", input_terms, onehot_rows(up_row, block_rows), precision=highest
    )
    in_grad = lax.psum_scatter(
        input_slab.reshape(tokens_here, width).astype(jnp.bfloat16),
        "col",
        scatter_dimension=1,
        tiled=True,
    )
    input_rows, cotan_rows = (
        lax.all_to_all(input_full, "row", split_axis=1, concat_axis=0, tiled=True),
        lax.all_to_all(cotan_full, "row", split_axis=1, concat_axis=0, tiled=True),
    )
    pre_rows, act_rows = (
        lax.all_gather(pre_grad.reshape(tokens_here, per_slab * side), "row", axis=0, tiled=True),
        lax.all_gather(act_low.reshape(tokens_here, per_slab * side), "row", axis=0, tiled=True),
    )
    own_up = up_index[0, 0]
    own_up_valid = (own_up >= 0).astype(jnp.float32)
    own_up_place = jnp.maximum(own_up, 0)
    own_down = down_index[0, 0]
    own_down_valid = (own_down >= 0).astype(jnp.float32)
    own_down_place = jnp.maximum(own_down, 0)
    input_own = jnp.take(input_rows.reshape(-1, per_row, side), own_up_place // per_slab, axis=1)
    pre_own = jnp.take(pre_rows.reshape(-1, per_slab, side), own_up_place % per_slab, axis=1)
    grad_upper = (
        jnp.einsum("tsk,tsn->skn", input_own, pre_own, preferred_element_type=jnp.float32)
        * scale
        * own_up_valid[:, None, None]
    )
    act_own = jnp.take(act_rows.reshape(-1, per_slab, side), own_down_place // per_row, axis=1)
    cotan_own = jnp.take(cotan_rows.reshape(-1, per_row, side), own_down_place % per_row, axis=1)
    grad_lower = (
        jnp.einsum("tsi,tsj->sij", act_own, cotan_own, preferred_element_type=jnp.float32)
        * scale
        * own_down_valid[:, None, None]
    )
    summed_upper, summed_lower = (
        lax.psum_scatter(
            grad_upper[None, None].astype(jnp.bfloat16), "dp", scatter_dimension=2, tiled=True
        ).astype(jnp.float32),
        lax.psum_scatter(
            grad_lower[None, None].astype(jnp.bfloat16), "dp", scatter_dimension=2, tiled=True
        ).astype(jnp.float32),
    )
    return (in_grad, summed_upper.astype(jnp.bfloat16), summed_lower.astype(jnp.bfloat16))


def solution(mesh):
    placed = (
        P(("dp", "row"), "col"),
        P(("dp", "row"), "col"),
        P("row", "col", None, None, None),
        P("row", "col", None),
        P("row", "col", None, None, None),
        P("row", "col", None),
    )
    return jax.shard_map(
        body,
        mesh=mesh,
        in_specs=placed,
        out_specs=(
            P(("dp", "row"), "col"),
            P("row", "col", "dp", None, None),
            P("row", "col", "dp", None, None),
        ),
        check_vma=False,
    )
```

profile of v0, /device:TPU:1, one launch (start us, length us, event | category | flops | bytes accessed | tf_op | source)
XLA Modules:
  0.0 507.8 jit_solution(1562803202395014537)
XLA Ops:
  7.2 0.7 all-gather.11.cloned.1.call-update
  7.9 0.7 all-gather.9.cloned.1.call-update
  8.7 0.7 all-gather.5.cloned.1.call-update
  10.0 8.6 %all_gather.26 = s32[4,1,16]{2,1,0:T(1,128)S(1)} all-gather(s32[1,1,16]{2,1,0:T(1,128)} %param.15), channel_id=1, replica_groups=mesh['dp'=4,'row'=4,'col'=32] {'row'}, dimensions={0}, use_global_device_ids=true | all-gather | bytes 320 | tf_op jit(solution)/shard_map/all_gather | solution.py:73
  18.6 5.4 %all_gather.28 = s32[4,1,16]{2,1,0:T(1,128)S(1)} all-gather(s32[1,1,16]{2,1,0:T(1,128)} %param.17), channel_id=1, replica_groups=mesh['dp'=4,'row'=4,'col'=32] {'row'}, dimensions={0}, use_global_device_ids=true | all-gather | bytes 320 | tf_op jit(solution)/shard_map/all_gather | solution.py:75
  25.0 0.7 compare_and_fusion.3
  26.4 0.7 compare_and_fusion.1
  27.0 60.2 %all-gather.11.cloned.1.call-done = bf16[128,6144]{0,1:T(8,128)(2,1)} async-done(((bf16[128,192]{0,1:T(8,128)(2,1)}), bf16[128,6144]{0,1:T(8,128)(2,1)}) %all-gather.11.cloned.1.call-update) | async-done | bytes 1572880 | tf_op jit(solution)/shard_map/all_gather | solution.py:55
  87.3 1.9 copy.75
  89.2 68.5 %all-gather.9.cloned.1.call-done = bf16[128,6144]{0,1:T(8,128)(2,1)} async-done(((bf16[128,192]{0,1:T(8,128)(2,1)}), bf16[128,6144]{0,1:T(8,128)(2,1)}) %all-gather.9.cloned.1.call-update) | async-done | bytes 1572880 | tf_op jit(solution)/shard_map/all_gather | solution.py:56
  157.7 1.9 copy.72
  159.6 4.4 all-to-all-start
  163.9 2.1 gather_fusion.2
  166.1 2.1 gather_fusion.1
  168.2 34.2 %all-gather.5.cloned.1.call-done = bf16[4,1,16,128,128]{4,3,2,1,0:T(8,128)(2,1)} async-done(((bf16[1,1,16,128,128]{4,3,2,1,0:T(8,128)(2,1)}), bf16[4,1,16,128,128]{4,3,2,1,0:T(8,128)(2,1)}) %all-gather.5.cloned.1.call-update) | async-done | bytes 2097168 | tf_op jit(solution)/shard_map/all_gather | solution.py:72
  202.4 1.9 bitcast_multiply_fusion.1
  204.6 3.6 convolution_bitcast_fusion.1
  208.2 5.4 %copy.77 = f32[128,64,128]{2,1,0:T(8,128)} copy(f32[128,64,128]{0,2,1:T(8,128)} %convolution_bitcast_fusion.1) | data formatting | bytes 8388608 | tf_op jit(solution)/shard_map/tsk,skn->tsn/transpose | solution.py:67
  213.6 24.2 %all-gather.7.cloned.1.call-done = bf16[4,1,16,128,128]{4,3,2,1,0:T(8,128)(2,1)} async-done(((bf16[1,1,16,128,128]{4,3,2,1,0:T(8,128)(2,1)}), bf16[4,1,16,128,128]{4,3,2,1,0:T(8,128)(2,1)}) %all-gather.7.cloned.1.call-update) | async-done | bytes 2097168 | tf_op jit(solution)/shard_map/all_gather | solution.py:74
  237.8 1.9 bitcast_multiply_fusion
  240.0 3.6 convolution_bitcast_fusion.2
  243.6 5.4 %copy.73 = f32[128,64,128]{2,1,0:T(8,128)} copy(f32[128,64,128]{0,2,1:T(8,128)} %convolution_bitcast_fusion.2) | data formatting | bytes 8388608 | tf_op jit(solution)/shard_map/tsj,sij->tsi/transpose | solution.py:85
  249.0 3.8 fusion.73
  252.8 1.5 fusion.70
  254.8 4.4 all-to-all-start.1
  259.2 32.5 %all_gather.32 = bf16[512,768]{0,1:T(8,128)(2,1)} all-gather(bf16[128,768]{0,1:T(8,128)(2,1)S(1)} %bitcast.157), channel_id=1, replica_groups=mesh['dp'=4,'row'=4,'col'=32] {'row'}, dimensions={0}, use_global_device_ids=true | all-gather | bytes 983040 | tf_op jit(solution)/shard_map/all_gather | solution.py:110
  291.7 1.5 copy.84
  293.2 2.1 gather_fusion.4
  295.4 8.5 %copy.81 = bf16[4,128,1536]{1,0,2:T(4,128)(2,1)} copy(bf16[4,128,1536]{1,2,0:T(8,128)(2,1)} %bitcast.22) | data formatting | bytes 3145728 | tf_op jit(solution)/shard_map/all_to_all | solution.py:106
  303.9 3.6 reshape.236
  307.5 2.7 copy.82
  310.2 3.5 gather_fusion.3
  313.7 4.0 fusion.44
  318.0 15.0 %all_gather.33 = bf16[512,768]{0,1:T(8,128)(2,1)} all-gather(bf16[128,768]{0,1:T(8,128)(2,1)S(1)} %bitcast.158), channel_id=1, replica_groups=mesh['dp'=4,'row'=4,'col'=32] {'row'}, dimensions={0}, use_global_device_ids=true | all-gather | bytes 983040 | tf_op jit(solution)/shard_map/all_gather | solution.py:111
  333.0 1.5 copy.87
  334.5 2.1 gather_fusion.5
  336.7 8.5 %copy.88 = bf16[4,128,1536]{1,0,2:T(4,128)(2,1)} copy(bf16[4,128,1536]{1,2,0:T(8,128)(2,1)} %bitcast.36) | data formatting | bytes 3145728 | tf_op jit(solution)/shard_map/all_to_all | solution.py:107
  345.2 3.7 reshape.241
  348.9 2.6 copy.89
  351.5 3.5 gather_fusion.6
  355.0 4.0 fusion.49
  359.3 2.1 gather_fusion
  361.5 5.2 %convolution_bitcast_fusion = f32[128,64,128]{0,2,1:T(8,128)} fusion(bf16[64,128,128]{2,1,0:T(8,128)(2,1)S(1)} %bitcast_multiply_fusion.1, bf16[64,128,128]{2,1,0:T(8,128)(2,1)} %gather_fusion, pred[64]{0:T(512)(128)(4,1)S(1)} %get-tuple-element.18), kind=kOutput, calls=%fused_computation.7 | convolution fusion | flops 269484032 | bytes 8388672 | tf_op jit(solution)/shard_map/tsn,skn->tsk/dot_general | solution.py:93
  366.6 5.4 %copy.79 = f32[128,64,128]{2,1,0:T(8,128)} copy(f32[128,64,128]{0,2,1:T(8,128)} %convolution_bitcast_fusion) | data formatting | bytes 8388608 | tf_op jit(solution)/shard_map/tsn,skn->tsk/transpose | solution.py:93
  372.0 4.3 fusion.23
  376.4 1.9 copy.94
  378.3 11.5 %reduce-scatter.8.cloned.1.call-done = bf16[1,1,4,128,128]{4,3,2,1,0:T(8,128)(2,1)} async-done(((bf16[1,1,16,128,128]{4,3,2,1,0:T(8,128)(2,1)}), bf16[1,1,4,128,128]{4,3,2,1,0:T(8,128)(2,1)}) %reduce-scatter.8.cloned.1.call-update) | async-done | bytes 131088 | tf_op jit(solution)/shard_map/reduce_scatter | solution.py:137
  389.8 111.1 %reduce-scatter.4.cloned.1.call-done = bf16[128,192]{0,1:T(8,128)(2,1)} async-done(((bf16[128,6144]{0,1:T(8,128)(2,1)}), bf16[128,192]{0,1:T(8,128)(2,1)}) %reduce-scatter.4.cloned.1.call-update) | async-done | bytes 49168 | tf_op jit(solution)/shard_map/reduce_scatter | solution.py:99
  (51 shorter events, 4.0 us)
Async XLA Ops:
  7.2 80.1 %all-gather.11.cloned.1.call-start = ((), (), s32[]{:S(2)}) async-start(), calls=%async_computation.8 | async-start | bytes 1622016 | tf_op jit(solution)/shard_map/all_gather | solution.py:55
  7.9 149.8 %all-gather.9.cloned.1.call-start = ((), (), s32[]{:S(2)}) async-start(), calls=%async_computation.7 | async-start | bytes 1622016 | tf_op jit(solution)/shard_map/all_gather | solution.py:56
  8.6 193.7 %all-gather.5.cloned.1.call-start = ((), (), s32[]{:S(2)}) async-start(), calls=%async_computation.5 | async-start | bytes 2621440 | tf_op jit(solution)/shard_map/all_gather | solution.py:72
  9.4 228.4 %all-gather.7.cloned.1.call-start = ((), (), s32[]{:S(2)}) async-start(), calls=%async_computation.6 | async-start | bytes 2621440 | tf_op jit(solution)/shard_map/all_gather | solution.py:74
  159.6 95.2 %all-to-all-start = ((bf16[128,4,1536]{0,2,1:T(8,128)(2,1)}), bf16[128,4,1536]{0,2,1:T(8,128)(2,1)}, u32[]{:S(2)}, u32[]{:S(2)}) async-start(bf16[128,4,1536]{0,2,1:T(8,128)(2,1)} %bitcast.153), calls=%async_computation.1 | async-start | bytes 3145728 | tf_op jit(solution)/shard_map/all_to_all | solution.py:106
  202.4 2.2 copy-start.2
  237.8 2.2 copy-start.1
  249.0 3.8 copy-start
  254.8 81.9 %all-to-all-start.1 = ((bf16[128,4,1536]{0,2,1:T(8,128)(2,1)}), bf16[128,4,1536]{0,2,1:T(8,128)(2,1)}, u32[]{:S(2)}, u32[]{:S(2)}) async-start(bf16[128,4,1536]{0,2,1:T(8,128)(2,1)} %bitcast.151), calls=%async_computation.3 | async-start | bytes 3145728 | tf_op jit(solution)/shard_map/all_to_all | solution.py:107
  259.2 119.1 %reduce-scatter.6.cloned.1.call-start = ((), (), s32[]{:S(2)}) async-start(), calls=%async_computation.10 | async-start | bytes 655360 | tf_op jit(solution)/shard_map/reduce_scatter | solution.py:134
  313.7 4.1 copy-start.3
  317.7 72.0 %reduce-scatter.8.cloned.1.call-start = ((), (), s32[]{:S(2)}) async-start(), calls=%async_computation.11 | async-start | bytes 655360 | tf_op jit(solution)/shard_map/reduce_scatter | solution.py:137
  359.0 141.9 %reduce-scatter.4.cloned.1.call-start = ((), (), s32[]{:S(2)}) async-start(), calls=%async_computation.9 | async-start | bytes 1622016 | tf_op jit(solution)/shard_map/reduce_scatter | solution.py:99
Sparse Core Ops, SparseCore 0:
  10.1 77.1 all-gather.10
  89.4 68.2 all-gather.8
  159.8 42.5 all-gather.4
  204.3 33.4 all-gather.6
  317.9 28.4 reduce-scatter.5
  359.1 30.5 reduce-scatter.7
  393.1 107.7 reduce-scatter.3
where the time goes:
time: 511 us; the launch traced here: 508 us
  waiting for transfers between devices  312 us (61%)
  local copies, waits for them, and re-layouts  73.9 us (14%)
  blocking collectives  61.6 us (12%)
  matrix products  30 us (6%)
  between operations  14.3 us (3%)
  starting transfers between devices  9.21 us (2%)
  other arithmetic  6.44 us (1%)
    reduce_scatter x1, waiting for transfers between devices, body(): lax.psum_scatter(input_slab.reshape(tokens_here, width).astype(jnp.bfloat...  111 us
    all_gather x1, waiting for transfers between devices, body(): lax.all_gather(out_grad, 'col', axis=1, tiled=True)  68.5 us
    all_gather x1, waiting for transfers between devices, body(): lax.all_gather(inputs, 'col', axis=1, tiled=True)  60.2 us
    all_gather x1, waiting for transfers between devices, body(): lax.all_gather(up_blocks, 'row', axis=0, tiled=True)  34.2 us
    all_gather x1, blocking collectives, body(): lax.all_gather(pre_grad.reshape(tokens_here, per_slab * side), 'row', axi...  32.5 us
    all_gather x1, waiting for transfers between devices, body(): lax.all_gather(down_blocks, 'row', axis=0, tiled=True)  24.2 us
    all_gather x1, blocking collectives, body(): lax.all_gather(act_low.reshape(tokens_here, per_slab * side), 'row', axis...  15 us
    reduce_scatter x1, waiting for transfers between devices, body(): lax.psum_scatter(grad_lower[None, None].astype(jnp.bfloat16), 'dp', scatt...  11.5 us
  transfers between devices with their start and end apart: 9, of which 6 were waited for; matrix products, arithmetic and copies ran while one was open for 22% of the time, Pallas kernels for 0%

commit v1 on v0

v1 whole, which is shorter than its diff:
```python
import functools
import math

import jax
import jax.numpy as jnp
from jax import lax
from jax.experimental import pallas as pl
from jax.experimental.pallas import tpu as pltpu
from jax.sharding import PartitionSpec as P

MESH = pl.DeviceIdType.MESH
BF = jnp.bfloat16
F32 = jnp.float32
ROOT = math.sqrt(2.0 / math.pi)

BLK = 128
CAP = 16
KR = 12
NC = 6
HALF = 64
PB = 3

DIRECT = 8


def tree(count, twos):
    strides = [2] * twos + [1] * (count - 2 * twos)
    marks = [0]
    for step in strides:
        marks.append(marks[-1] + step)
    return strides, marks


def gelu_parts(value):
    inner = ROOT * (value + 0.044715 * value * value * value)
    tanh_inner = jnp.tanh(inner)
    result = 0.5 * value * (1.0 + tanh_inner)
    slope = 0.5 * (1.0 + tanh_inner) + 0.5 * value * (
        1.0 - tanh_inner * tanh_inner
    ) * ROOT * (1.0 + 3.0 * 0.044715 * value * value)
    return result, slope


def nt_dot(a, b):
    return lax.dot_general(a, b, (((1,), (1,)), ((), ())), preferred_element_type=F32)


def kernel(
    sizes,
    x_ref, g_ref, wu_hbm, ui_ref, wd_hbm, di_ref,
    in_ref, up_ref, down_ref,
    xb, gb, wub, wdb, meta_v, meta_s, half_in, p_ref, a_ref, pg_ref, act_t, pg_t,
    dwd, dwu, sdown, sup, rdown, rup, rdown2, rup2,
    own, mine, theirs, ring_out, ring_leaf, ring_bone, fin, fin_in,
    half_s, half_r, meta_ss, meta_r, meta_l, wsend, whelp, wrecv, wlocal,
    ag_s, ag_r, sib_s, sib_r,
    d1_s, d1_r, u1_s, u1_r, d2_s, d2_r, u2_s, u2_r,
    part_s, part_r, ring_s, leaf_r, bone_r, fin_s, fin_r,
):
    nd, nr, nz = sizes
    scale = 1.0 / math.sqrt(nd * nr * 2 * HALF)
    xg, wb = (xb, gb), (wub, wdb)
    d, r, c = lax.axis_index("dp"), lax.axis_index("row"), lax.axis_index("col")
    z, h = c // 2, c % 2
    o = 1 - h
    sibling = (d, r, z * 2 + o)
    n_of = {1: nz // 2, -1: nz // 2 - 1}

    def xpeer(k):
        return (d, lax.rem(r + k, nr), c)

    def ypeer(k):
        return (lax.rem(d + k, nd), r, c)

    def zpeer(k):
        return (d, r, lax.rem(z + nz + k, nz) * 2 + h)

    def send(src, dst, ss, rs, to):
        copy = pltpu.make_async_remote_copy(
            src_ref=src, dst_ref=dst, send_sem=ss, recv_sem=rs, device_id=to, device_id_type=MESH
        )
        copy.start()

    def drain(ref, sem):
        pltpu.make_async_copy(ref, ref, sem).wait()

    partners = [sibling] + [zpeer(k) for k in (1, -1, 2, -2)]
    partners += [xpeer(k) for k in range(1, nr)] + [ypeer(k) for k in range(1, nd)]
    barrier = pltpu.get_barrier_semaphore()
    for to in partners:
        pl.semaphore_signal(barrier, inc=1, device_id=to, device_id_type=MESH)
    pl.semaphore_wait(barrier, len(partners))

    mine_rows = pl.ds(pl.multiple_of(h * HALF, HALF), HALF)
    their_rows = pl.ds(pl.multiple_of(o * HALF, HALF), HALF)
    srcs = (x_ref, g_ref)
    for a in range(2):
        send(srcs[a].at[their_rows], half_in.at[a], half_s.at[a], half_r.at[a], sibling)

    lane = lax.broadcasted_iota(jnp.int32, (8, BLK), 1)
    line = lax.broadcasted_iota(jnp.int32, (8, BLK), 0)
    table = jnp.where(line >= 6, nr * CAP, 0)
    for s in range(CAP):
        up = ui_ref[0, 0, s]
        down = di_ref[0, 0, s]
        up_ok, down_ok = up >= 0, down >= 0
        up_p, down_p = jnp.maximum(up, 0), jnp.maximum(down, 0)
        entries = (
            r * KR + up_p // NC, up_p % NC, up_ok.astype(jnp.int32),
            down_p // KR, r * KR + down_p % KR, down_ok.astype(jnp.int32),
        )
        for i, entry in enumerate(entries):
            table = jnp.where((line == i) & (lane == s), entry, table)
        table = jnp.where((line == 6) & (lane == up), r * CAP + s, table)
        table = jnp.where((line == 7) & (lane == down), r * CAP + s, table)
    meta_v[r] = table
    for k in range(1, nr):
        send(meta_v.at[r], meta_v.at[r], meta_ss.at[k], meta_r.at[k], xpeer(k))

    for a in range(2):
        drain(half_in.at[a], half_r.at[a])
        kept = srcs[a][mine_rows, :]
        other = half_in[a]

        def place(low, high, a=a):
            whole = jnp.concatenate([low, high], axis=1)
            for i in range(PB):
                xg[a][PB * z + i, mine_rows, :] = whole[:, i * BLK:(i + 1) * BLK]

        @pl.when(h == 0)
        def _(kept=kept, other=other, place=place):
            place(kept, other)

        @pl.when(h == 1)
        def _(kept=kept, other=other, place=place):
            place(other, kept)

    def piece(a, k, rows=mine_rows):
        where = lax.rem(z + nz + k, nz)
        return xg[a].at[pl.ds(PB * where, PB), rows, :]

    def share(a, k):
        send(piece(a, k), piece(a, k), sib_s.at[a], sib_r.at[a], sibling)

    def gather_send(a, way, at, hop):
        ref = piece(a, -way * at)
        side = 0 if way == 1 else 1
        send(ref, ref, ag_s.at[a], ag_r.at[a, side, at + hop - 1], zpeer(way * hop))

    def gather_wait(a, way, at):
        side = 0 if way == 1 else 1
        drain(piece(a, -way * at), ag_r.at[a, side, at - 1])

    trees = {way: tree(n_of[way], n_of[way] // 2) for way in (1, -1)}

    def gather_step(a, way, j):
        strides, marks = trees[way]
        if j > len(strides):
            return
        at = marks[j]
        if j > 0:
            gather_wait(a, way, at)
        if j < len(strides):
            gather_send(a, way, at, strides[j])
            if strides[j] == 2:
                gather_send(a, way, at, 1)
        if j > 0:
            share(a, -way * at)
            if strides[j - 1] == 2:
                gather_wait(a, way, at - 1)
                share(a, -way * (at - 1))

    for a in range(2):
        for way in (1, -1):
            gather_step(a, way, 0)
        share(a, 0)

    srcw = (wu_hbm.at[0, 0], wd_hbm.at[0, 0])
    per = (CAP - DIRECT) // nd
    for a in range(2):
        for k in range(1, nr):
            send(
                srcw[a].at[pl.ds(per * d, per)], wb[a].at[pl.ds(CAP * r + per * d, per)],
                wsend.at[a], whelp.at[a, k], xpeer(k),
            )
    for a in range(2):
        for k in range(1, nr):
            send(
                srcw[a].at[pl.ds(CAP - DIRECT, DIRECT)],
                wb[a].at[pl.ds(CAP * r + CAP - DIRECT, DIRECT)],
                wsend.at[a], wrecv.at[a], xpeer(k),
            )
    locals_ = [
        pltpu.make_async_copy(srcw[a], wb[a].at[pl.ds(CAP * r, CAP)], wlocal.at[a]) for a in range(2)
    ]
    for copy in locals_:
        copy.start()
    for a in range(2):
        wb[a][nr * CAP] = jnp.zeros((BLK, BLK), BF)

    def help_on(a):
        for k in range(1, nr):
            src = lax.rem(r + nr - k, nr)
            ref = wb[a].at[pl.ds(CAP * src + per * d, per)]
            drain(ref, whelp.at[a, k])
            for ky in range(1, nd):
                send(ref, ref, wsend.at[a], wrecv.at[a], ypeer(ky))

    longest = max(len(trees[way][0]) for way in (1, -1))
    for j in range(1, longest + 1):
        for a in range(2):
            for way in (1, -1):
                gather_step(a, way, j)
        if j <= 2:
            help_on(j - 1)

    for k in range(1, nr):
        src = lax.rem(r + nr - k, nr)
        drain(meta_v.at[src], meta_r.at[k])
    to_smem = pltpu.make_async_copy(meta_v, meta_s, meta_l)
    to_smem.start()
    to_smem.wait()

    for a in range(2):
        drain(xg[a].at[:, pl.ds(0, HALF), :], sib_r.at[a])
    def weights_here(a):
        locals_[a].wait()
        got = (nr - 1) * DIRECT + (nr - 1) * (nd - 1) * per
        drain(wb[a].at[pl.ds(0, got)], wrecv.at[a])

    weights_here(0)
    step_rows = 4
    steps = nr * KR // step_rows
    per_owner = KR // step_rows
    p_ref[...] = jnp.zeros_like(p_ref)
    a_ref[...] = jnp.zeros_like(a_ref)

    @pl.loop(0, steps)
    def _(t):
        owner, base = t // per_owner, (t % per_owner) * step_rows
        left = jnp.concatenate([xb[step_rows * t + i] for i in range(step_rows)], axis=1)
        right = jnp.concatenate(
            [
                jnp.concatenate(
                    [wub[meta_s[owner, 6, (base + i) * NC + j]] for j in range(NC)], axis=1
                )
                for i in range(step_rows)
            ],
            axis=0,
        )
        p_ref[...] += jnp.dot(left, right, preferred_element_type=F32)

    act, slope = gelu_parts(p_ref[...])
    act_low = act.astype(BF)
    p_ref[...] = slope
    for i in range(NC):
        act_t[i] = act_low[:, i * BLK:(i + 1) * BLK].T

    def down_terms(owner):
        @pl.loop(0, CAP // 4)
        def _(t):
            for u in range(4):
                s = 4 * t + u
                i, j = meta_s[owner, 3, s], meta_s[owner, 4, s]
                keep = meta_s[owner, 5, s].astype(F32) * scale
                term = jnp.dot(act_t[i], gb[j], preferred_element_type=F32)
                dwd[owner, s] = (term * keep).astype(BF)

    for k in (2, 1, 3):
        owner = lax.rem(r + k, nr)
        down_terms(owner)
        send(dwd.at[owner], rdown.at[k - 1], d1_s, d1_r.at[k - 1], xpeer(k))
    down_terms(r)

    weights_here(1)

    @pl.loop(0, steps)
    def _(t):
        owner, base = t // per_owner, (t % per_owner) * step_rows
        left = jnp.concatenate([gb[step_rows * t + i] for i in range(step_rows)], axis=1)
        right = jnp.concatenate(
            [
                jnp.concatenate(
                    [wdb[meta_s[owner, 7, i * KR + base + j]] for j in range(step_rows)], axis=1
                )
                for i in range(NC)
            ],
            axis=0,
        )
        a_ref[...] += nt_dot(left, right)

    pre_grad = (a_ref[...] * p_ref[...]).astype(BF)
    for i in range(NC):
        pg_t[i] = pre_grad[:, i * BLK:(i + 1) * BLK].T
    pg_ref[0:HALF, :] = pre_grad[0:HALF, :]
    pg_ref[HALF:2 * HALF, :] = pre_grad[HALF:2 * HALF, :]
    pg_ordered = jnp.concatenate([pg_ref[mine_rows, :], pg_ref[their_rows, :]], axis=0)
    pg_ref[...] = pg_ordered

    def up_terms(owner_y):
        @pl.loop(0, nr)
        def _(owner):
            for u in range(CAP // nd):
                s = (CAP // nd) * owner_y + u
                k, j = meta_s[owner, 0, s], meta_s[owner, 1, s]
                keep = meta_s[owner, 2, s].astype(F32) * scale
                term = jnp.dot(pg_t[j], xb[k], preferred_element_type=F32)
                dwu[owner, s] = (term * keep).astype(BF)

    share_y = CAP // nd
    for k in (2, 1, 3):
        owner_y = lax.rem(d + k, nd)
        up_terms(owner_y)
        send(
            dwu.at[:, pl.ds(share_y * owner_y, share_y)], rup.at[k - 1], u1_s, u1_r.at[k - 1], ypeer(k)
        )
    up_terms(d)

    def partial_piece(index, k):
        where = lax.rem(z + nz + k, nz)
        owner = where // (KR // PB)
        base = (where % (KR // PB)) * PB
        right = jnp.concatenate(
            [
                jnp.concatenate(
                    [wub[meta_s[owner, 6, (base + i) * NC + j]] for j in range(NC)], axis=1
                )
                for i in range(PB)
            ],
            axis=0,
        )
        both = nt_dot(pg_ref[...], right)
        for i in range(PB):
            own[index, i] = both[0:HALF, i * BLK:(i + 1) * BLK]
            mine[index, i] = both[HALF:2 * HALF, i * BLK:(i + 1) * BLK].astype(BF)
        send(mine.at[index], theirs.at[index], part_s, part_r.at[index], sibling)

    n_right, n_left = n_of[1], n_of[-1]

    def index_of(way, at):
        return at - 1 if way == 1 else n_right + at - 1

    order = []
    for at in range(n_right, 0, -1):
        order.append((1, at))
        if at <= n_left:
            order.append((-1, at))
    for way, at in order:
        partial_piece(index_of(way, at), way * at)
    partial_piece(nz - 1, 0)

    def summed(index, extra):
        drain(theirs.at[index], part_r.at[index])
        total = own[index] + theirs[index].astype(F32)
        for ref in extra:
            total = total + ref[...].astype(F32)
        return total

    def incoming(way, at):
        strides, marks = trees[way]
        side = 0 if way == 1 else 1
        refs = []
        j = marks.index(at)
        if j < len(strides):
            if strides[j] == 2:
                refs.append((ring_leaf.at[side, at], leaf_r.at[side, at]))
            refs.append((ring_bone.at[side, at], bone_r.at[side, at]))
        return refs

    def ring_step(way, at):
        strides, marks = trees[way]
        side = 0 if way == 1 else 1
        index = index_of(way, at)
        if at in marks:
            refs = incoming(way, at)
            for ref, sem in refs:
                drain(ref, sem)
            total = summed(index, [ref for ref, _ in refs])
            hop = strides[marks.index(at) - 1]
            ring_out[index] = total.astype(BF)
            send(
                ring_out.at[index], ring_bone.at[side, at - hop], ring_s, bone_r.at[side, at - hop],
                zpeer(way * hop),
            )
        else:
            ring_out[index] = summed(index, []).astype(BF)
            send(
                ring_out.at[index], ring_leaf.at[side, at - 1], ring_s, leaf_r.at[side, at - 1],
                zpeer(way * 1),
            )

    def waits(way, at):
        marks = trees[way][1]
        return at in marks[:-1]

    for way, at in order:
        if not waits(way, at):
            ring_step(way, at)
    for way, at in order:
        if waits(way, at):
            ring_step(way, at)

    refs = incoming(1, 0) + incoming(-1, 0)
    for ref, sem in refs:
        drain(ref, sem)
    total = summed(nz - 1, [ref for ref, _ in refs])
    flat = jnp.concatenate([total[i] for i in range(PB)], axis=1).astype(BF)
    width = x_ref.shape[1]
    fin[0] = flat[:, 0:width]
    fin[1] = flat[:, width:2 * width]
    send(fin.at[o], fin_in, fin_s, fin_r, sibling)
    in_ref[mine_rows, :] = fin[h]
    drain(fin_in, fin_r)
    in_ref[their_rows, :] = fin_in[...]

    for k in range(1, nr):
        drain(rdown.at[k - 1], d1_r.at[k - 1])

    @pl.loop(0, CAP)
    def _(s):
        total = dwd[r, s].astype(F32)
        for k in range(nr - 1):
            total += rdown[k, s].astype(F32)
        sdown[s] = total.astype(BF)

    for k in (2, 1, 3):
        owner_y = lax.rem(d + k, nd)
        send(
            sdown.at[pl.ds(share_y * owner_y, share_y)], rdown2.at[k - 1], d2_s, d2_r.at[k - 1], ypeer(k)
        )

    for k in range(1, nd):
        drain(rup.at[k - 1], u1_r.at[k - 1])

    @pl.loop(0, nr)
    def _(owner):
        for u in range(share_y):
            total = dwu[owner, share_y * d + u].astype(F32)
            for k in range(nd - 1):
                total += rup[k, owner, u].astype(F32)
            sup[owner, u] = total.astype(BF)

    for k in (2, 1, 3):
        owner = lax.rem(r + k, nr)
        send(sup.at[owner], rup2.at[k - 1], u2_s, u2_r.at[k - 1], xpeer(k))

    for k in range(1, nd):
        drain(rdown2.at[k - 1], d2_r.at[k - 1])
    for u in range(share_y):
        total = sdown[share_y * d + u].astype(F32)
        for k in range(nd - 1):
            total += rdown2[k, u].astype(F32)
        down_ref[0, 0, u] = total.astype(BF)

    for k in range(1, nr):
        drain(rup2.at[k - 1], u2_r.at[k - 1])
    for u in range(share_y):
        total = sup[r, u].astype(F32)
        for k in range(nr - 1):
            total += rup2[k, u].astype(F32)
        up_ref[0, 0, u] = total.T.astype(BF)

    for a in range(2):
        drain(half_in.at[a], half_s.at[a])
        drain(xg[a].at[pl.ds(0, PB * (nz - 1)), pl.ds(0, HALF), :], ag_s.at[a])
        drain(xg[a].at[:, pl.ds(0, HALF), :], sib_s.at[a])
        gone = (nr - 1) * (per + DIRECT) + (nr - 1) * (nd - 1) * per
        drain(wb[a].at[pl.ds(0, gone)], wsend.at[a])
    for k in range(1, nr):
        drain(meta_v.at[r], meta_ss.at[k])
    drain(rdown, d1_s)
    drain(rup, u1_s)
    drain(rdown2, d2_s)
    drain(rup2, u2_s)
    drain(mine, part_s)
    drain(ring_out, ring_s)
    drain(fin_in, fin_s)


def solution(mesh):
    nd, nr, nc = mesh.shape["dp"], mesh.shape["row"], mesh.shape["col"]
    nz = nc // 2
    DMA = pltpu.SemaphoreType.DMA
    VMEM = pltpu.VMEM

    def body(inputs, out_grad, up_blocks, up_index, down_blocks, down_index):
        tokens, width = inputs.shape
        blocks = nr * KR
        hidden = NC * BLK
        share = CAP // nd
        vmem = pl.BlockSpec(memory_space=pltpu.VMEM)
        smem = pl.BlockSpec(memory_space=pltpu.SMEM)
        hbm = pl.BlockSpec(memory_space=pl.ANY)
        scratch = [
            VMEM((blocks, tokens, BLK), BF),
            VMEM((blocks, tokens, BLK), BF),
            VMEM((nr * CAP + 1, BLK, BLK), BF),
            VMEM((nr * CAP + 1, BLK, BLK), BF),
            VMEM((nr, 8, BLK), jnp.int32),
            pltpu.SMEM((nr, 8, BLK), jnp.int32),
            VMEM((2, HALF, width), BF),
            VMEM((tokens, hidden), F32),
            VMEM((tokens, hidden), F32),
            VMEM((tokens, hidden), BF),
            VMEM((NC, BLK, tokens), BF),
            VMEM((NC, BLK, tokens), BF),
            VMEM((nr, CAP, BLK, BLK), BF),
            VMEM((nr, CAP, BLK, BLK), BF),
            VMEM((CAP, BLK, BLK), BF),
            VMEM((nr, share, BLK, BLK), BF),
            VMEM((nr - 1, CAP, BLK, BLK), BF),
            VMEM((nd - 1, nr, share, BLK, BLK), BF),
            VMEM((nd - 1, share, BLK, BLK), BF),
            VMEM((nr - 1, share, BLK, BLK), BF),
            VMEM((nz, PB, HALF, BLK), F32),
            VMEM((nz, PB, HALF, BLK), BF),
            VMEM((nz, PB, HALF, BLK), BF),
            VMEM((nz - 1, PB, HALF, BLK), BF),
            VMEM((2, nz // 2, PB, HALF, BLK), BF),
            VMEM((2, nz // 2, PB, HALF, BLK), BF),
            VMEM((2, HALF, width), BF),
            VMEM((HALF, width), BF),
            DMA((2,)), DMA((2,)),
            DMA((nr,)), DMA((nr,)), DMA,
            DMA((2,)), DMA((2, nr)), DMA((2,)), DMA((2,)),
            DMA((2,)), DMA((2, 2, nz // 2)),
            DMA((2,)), DMA((2,)),
            DMA, DMA((nr - 1,)), DMA, DMA((nd - 1,)),
            DMA, DMA((nd - 1,)), DMA, DMA((nr - 1,)),
            DMA, DMA((nz,)),
            DMA, DMA((2, nz // 2)), DMA((2, nz // 2)),
            DMA, DMA,
        ]
        return pl.pallas_call(
            functools.partial(kernel, (nd, nr, nz)),
            out_shape=(
                jax.ShapeDtypeStruct((tokens, width), BF),
                jax.ShapeDtypeStruct((1, 1, share, BLK, BLK), BF),
                jax.ShapeDtypeStruct((1, 1, share, BLK, BLK), BF),
            ),
            in_specs=[vmem, vmem, hbm, smem, hbm, smem],
            out_specs=(vmem, vmem, vmem),
            scratch_shapes=scratch,
            compiler_params=pltpu.CompilerParams(
                collective_id=0, has_side_effects=True, vmem_limit_bytes=48 << 20
            ),
        )(inputs, out_grad, up_blocks, up_index, down_blocks, down_index)

    return jax.shard_map(
        body,
        mesh=mesh,
        in_specs=(
            P(("dp", "row"), "col"),
            P(("dp", "row"), "col"),
            P("row", "col", None, None, None),
            P("row", "col", None),
            P("row", "col", None, None, None),
            P("row", "col", None),
        ),
        out_specs=(
            P(("dp", "row"), "col"),
            P("row", "col", "dp", None, None),
            P("row", "col", "dp", None, None),
        ),
        check_vma=False,
    )
```

time: 511 us -> 101 us (0.20)
  waiting for transfers between devices: 312 us -> 0 us
  Pallas kernels: 0 us -> 94.7 us
  local copies, waits for them, and re-layouts: 73.9 us -> 5.68 us
  blocking collectives: 61.6 us -> 0 us
  matrix products: 30 us -> 0 us
  between operations: 14.3 us -> 0.69 us
  starting transfers between devices: 9.21 us -> 0 us
  other arithmetic: 6.44 us -> 0 us
    all_gather x4 -> x0, waiting for transfers between devices: 187 us -> none  [the longest x1 68.5 us: body(): lax.all_gather(out_grad, 'col', axis=1, tiled=True)]
    reduce_scatter x3 -> x0, waiting for transfers between devices: 123 us -> none  [the longest x1 111 us: body(): lax.psum_scatter(input_slab.reshape(tokens_here, width).astype(jnp.bfloat...]
    pallas_call x0 -> x1, Pallas kernels: none -> 94.7 us  [body(): pl.pallas_call(functools.partial(kernel, (nd, nr, nz)), out_shape=(jax.Sh...]
    all_gather x4 -> x0, blocking collectives: 61.6 us -> none  [the longest x1 32.5 us: body(): lax.all_gather(pre_grad.reshape(tokens_here, per_slab * side), 'row', axi...]
    dot_general x8 -> x0, matrix products: 30 us -> none  [the longest x1 5.18 us: body(): jnp.einsum('tsn,skn->tsk', pre_taken, up_matrix, preferred_element_type=j...]
    reshape x8 -> x0, local copies, waits for them, and re-layouts: 19.4 us -> none  [the longest x2 6.3 us: body(): input_rows.reshape(-1, per_row, side)]
    gather x7 -> x0, local copies, waits for them, and re-layouts: 17.7 us -> none  [the longest x1 3.53 us: body(): jnp.take(input_rows.reshape(-1, per_row, side), own_up_place // per_slab,...]
    all_to_all x2 -> x0, local copies, waits for them, and re-layouts: 17 us -> none  [the longest x1 8.51 us: body(): lax.all_to_all(cotan_full, 'row', split_axis=1, concat_axis=0, tiled=True)]
  transfers between devices with their start and end apart: 9 -> 0, of which waited for: 6 -> 0; matrix products, arithmetic and copies ran while one was open for 22% -> 0% of each run, Pallas kernels for 0% -> 0%
where the time goes in v1:
time: 101 us
  Pallas kernels  94.7 us (94%)
  local copies, waits for them, and re-layouts  5.68 us (6%)
    pallas_call x1, Pallas kernels, body(): pl.pallas_call(functools.partial(kernel, (nd, nr, nz)), out_shape=(jax.Sh...  94.7 us
    unnamed x14, local copies, waits for them, and re-layouts  4.96 us

profile of v1, /device:TPU:1, one launch (start us, length us, event | category | flops | bytes accessed | tf_op | source)
XLA Modules:
  0.0 101.1 jit_solution(2371287811939862304)
XLA Ops:
  0.6 0.0 copy-start.4
  0.6 0.9 copy.9.x_ref
  1.6 0.0 copy-done.4
  1.6 0.0 copy-start.2
  1.6 0.0 copy-start.3
  1.6 0.1 copy.10.g_ref
  1.7 0.5 copy-done.2
  2.2 0.0 copy-done.3
  2.2 0.0 copy-start
  2.2 1.0 %copy-done = bf16[1,1,16,128,128]{4,3,2,1,0:T(8,128)(2,1)S(1)} copy-done((bf16[1,1,16,128,128]{4,3,2,1,0:T(8,128)(2,1)S(1)}, bf16[1,1,16,128,128]{4,3,2,1,0:T(8,128)(2,1)}, u32[]{:S(2)}) %copy-start) | copy-done | bytes 524312
  3.3 0.0 copy-start.1
  3.3 1.0 %copy-done.1 = bf16[1,1,16,128,128]{4,3,2,1,0:T(8,128)(2,1)S(1)} copy-done((bf16[1,1,16,128,128]{4,3,2,1,0:T(8,128)(2,1)S(1)}, bf16[1,1,16,128,128]{4,3,2,1,0:T(8,128)(2,1)}, u32[]{:S(2)}) %copy-start.1) | copy-done | bytes 524312
  4.3 94.7 %shard_map.85 = (bf16[128,192]{1,0:T(8,128)(2,1)S(1)}, bf16[1,1,4,128,128]{4,3,2,1,0:T(8,128)(2,1)S(1)}, bf16[1,1,4,128,128]{4,3,2,1,0:T(8,128)(2,1)S(1)}) custom-call(bf16[128,192]{1,0:T(8,128)(2,1)S(1)} %copy.9.x_ref, bf16[128,192]{1,0:T(8,128)(2,1)S(1)} %copy.10.g_ref, bf16[1,1,16,128,128]{4,3,2,1,0:T(8,128)(2,1)S(1)} %copy-done, ...), custom_call_target="tpu_custom_call" | custom-call | tf_op jit(solution)/shard_map/pallas_call | solution.py:534
  99.1 0.7 copy.11
  99.8 0.7 copy.14
  100.4 0.7 copy.15
Async XLA Ops:
  0.6 0.9 copy-start.4
  1.6 0.7 copy-start.2
  1.6 0.7 copy-start.3
  2.2 1.0 %copy-start = (bf16[1,1,16,128,128]{4,3,2,1,0:T(8,128)(2,1)S(1)}, bf16[1,1,16,128,128]{4,3,2,1,0:T(8,128)(2,1)}, u32[]{:S(2)}) copy-start(bf16[1,1,16,128,128]{4,3,2,1,0:T(8,128)(2,1)} %wu_hbm.1) | copy-start | bytes 1572868
  3.3 1.0 %copy-start.1 = (bf16[1,1,16,128,128]{4,3,2,1,0:T(8,128)(2,1)S(1)}, bf16[1,1,16,128,128]{4,3,2,1,0:T(8,128)(2,1)}, u32[]{:S(2)}) copy-start(bf16[1,1,16,128,128]{4,3,2,1,0:T(8,128)(2,1)} %wd_hbm.1) | copy-start | bytes 1572868

commit v2 on v1

v2 whole, which is shorter than its diff:
```python
import functools
import math

import jax
import jax.numpy as jnp
from jax import lax
from jax.experimental import pallas as pl
from jax.experimental.pallas import tpu as pltpu
from jax.sharding import PartitionSpec as P

MESH = pl.DeviceIdType.MESH
BF = jnp.bfloat16
F32 = jnp.float32
ROOT = math.sqrt(2.0 / math.pi)

BLK = 128
CAP = 16
KR = 12
NC = 6
HALF = 64
GATHER_TWOS = 3
PB = 3

DIRECT = (8, 4)


def tree(count, twos):
    strides = [2] * twos + [1] * (count - 2 * twos)
    marks = [0]
    for step in strides:
        marks.append(marks[-1] + step)
    return strides, marks


def gelu_parts(value):
    inner = ROOT * (value + 0.044715 * value * value * value)
    tanh_inner = jnp.tanh(inner)
    result = 0.5 * value * (1.0 + tanh_inner)
    slope = 0.5 * (1.0 + tanh_inner) + 0.5 * value * (
        1.0 - tanh_inner * tanh_inner
    ) * ROOT * (1.0 + 3.0 * 0.044715 * value * value)
    return result, slope


def nt_dot(a, b):
    return lax.dot_general(a, b, (((1,), (1,)), ((), ())), preferred_element_type=F32)


def kernel(
    sizes,
    x_hbm, g_hbm, wu_hbm, ui_ref, wd_hbm, di_ref,
    in_ref, up_ref, down_ref,
    xb, gb, wub, wdb, meta_v, meta_s, p_ref, a_ref, s_ref, pg_t, act_t,
    dw00, dw01, dw10, dw11, relay_in, relayed, one_in, half_sum, two_in,
    own, mine, theirs, ring_out, ring_leaf, ring_bone,
    first_l, meta_ss, meta_r, meta_l, wsend, whelp, wrecv, wlocal,
    ag_s, ag_r, sib_s, sib_r, sib_all,
    one_s, relay_r, one_r, two_s, two_r,
    part_s, part_r, ring_s, leaf_r, bone_r,
):
    nd, nr, nz = sizes
    tokens = BLK
    third = x_hbm.shape[0]
    width = third * HALF
    wide = 2 * third
    scale = 1.0 / math.sqrt(nd * nr * tokens)
    xg, wb = (xb, gb), (wub, wdb)
    dw = ((dw00, dw01), (dw10, dw11))
    d, r, c = lax.axis_index("dp"), lax.axis_index("row"), lax.axis_index("col")
    z, h = c // 2, c % 2
    sibling = (d, r, z * 2 + 1 - h)
    n_of = {1: nz // 2, -1: nz // 2 - 1}

    def xpeer(k):
        return (d, lax.rem(r + k, nr), c)

    def ypeer(k):
        return (lax.rem(d + k, nd), r, c)

    def zpeer(k):
        return (d, r, lax.rem(z + nz + k, nz) * 2 + h)

    def send(src, dst, ss, rs, to):
        copy = pltpu.make_async_remote_copy(
            src_ref=src, dst_ref=dst, send_sem=ss, recv_sem=rs, device_id=to, device_id_type=MESH
        )
        copy.start()

    def drain(ref, sem):
        pltpu.make_async_copy(ref, ref, sem).wait()

    own_rows = pl.ds(third * c, third)
    srcs = (x_hbm, g_hbm)
    firsts = [pltpu.make_async_copy(srcs[a], xg[a].at[own_rows], first_l.at[a]) for a in range(2)]
    srcw = (wu_hbm.at[0, 0], wd_hbm.at[0, 0])
    locals_ = [
        pltpu.make_async_copy(srcw[a], wb[a].at[pl.ds(CAP * r, CAP)], wlocal.at[a]) for a in range(2)
    ]
    for copy in firsts + locals_:
        copy.start()

    partners = [sibling] + [zpeer(k) for k in (1, -1, 2, -2)]
    partners += [xpeer(k) for k in range(1, nr)] + [ypeer(k) for k in range(1, nd)]
    barrier = pltpu.get_barrier_semaphore()
    for to in partners:
        pl.semaphore_signal(barrier, inc=1, device_id=to, device_id_type=MESH)

    pl.semaphore_wait(barrier, len(partners))

    def piece(a, k, core):
        where = lax.rem(z + nz + k, nz)
        return xg[a].at[pl.ds(wide * where + third * core, third)]

    def share(a, way, at):
        ref = piece(a, -way * at, h)
        arrived = sib_r.at[2 * at - 1 if way == 1 else 2 * at] if a == 0 else sib_all
        send(ref, ref, sib_s.at[a], arrived, sibling)

    trees = {way: tree(n_of[way], min(GATHER_TWOS, n_of[way] // 2)) for way in (1, -1)}

    def gather_send(a, way, at, hop):
        ref = piece(a, -way * at, h)
        side = 0 if way == 1 else 1
        send(ref, ref, ag_s.at[a], ag_r.at[a, side, at + hop - 1], zpeer(way * hop))

    def gather_wait(a, way, at):
        side = 0 if way == 1 else 1
        drain(piece(a, -way * at, h), ag_r.at[a, side, at - 1])

    def gather_step(a, way, j):
        strides, marks = trees[way]
        if j > len(strides):
            return
        at = marks[j]
        if j > 0:
            gather_wait(a, way, at)
        if j < len(strides):
            gather_send(a, way, at, strides[j])
            if strides[j] == 2:
                gather_send(a, way, at, 1)
        if j > 0:
            share(a, way, at)

    def gather_leaf(a, way, j):
        strides, marks = trees[way]
        if 0 < j <= len(strides) and strides[j - 1] == 2:
            gather_wait(a, way, marks[j] - 1)
            share(a, way, marks[j] - 1)

    for a in range(2):
        firsts[a].wait()
        for way in (1, -1):
            gather_step(a, way, 0)
    for a in range(2):
        share(a, -1, 0)

    per = [(CAP - direct) // nd for direct in DIRECT]

    def weights_help(a):
        for k in range(1, nr):
            send(
                srcw[a].at[pl.ds(per[a] * d, per[a])], wb[a].at[pl.ds(CAP * r + per[a] * d, per[a])],
                wsend.at[a], whelp.at[a, k], xpeer(k),
            )

    def weights_direct(a):
        for k in range(1, nr):
            send(
                srcw[a].at[pl.ds(CAP - DIRECT[a], DIRECT[a])],
                wb[a].at[pl.ds(CAP * r + CAP - DIRECT[a], DIRECT[a])],
                wsend.at[a], wrecv.at[a], xpeer(k),
            )

    weights_help(0)
    weights_help(1)
    weights_direct(0)

    lane = lax.broadcasted_iota(jnp.int32, (8, BLK), 1)
    line = lax.broadcasted_iota(jnp.int32, (8, BLK), 0)

    def publish():
        table = jnp.where(line >= 6, nr * CAP, 0)
        for s in range(CAP):
            up = ui_ref[0, 0, s]
            down = di_ref[0, 0, s]
            up_ok, down_ok = up >= 0, down >= 0
            up_p, down_p = jnp.maximum(up, 0), jnp.maximum(down, 0)
            entries = (
                r * KR + up_p // NC, up_p % NC, up_ok.astype(jnp.int32),
                down_p // KR, r * KR + down_p % KR, down_ok.astype(jnp.int32),
            )
            for i, entry in enumerate(entries):
                table = jnp.where((line == i) & (lane == s), entry, table)
            table = jnp.where((line == 6) & (lane == up), r * CAP + s, table)
            table = jnp.where((line == 7) & (lane == down), r * CAP + s, table)
        meta_v[r] = table
        for k in range(1, nr):
            send(meta_v.at[r], meta_v.at[r], meta_ss.at[k], meta_r.at[k], xpeer(k))
        for a in range(2):
            wb[a][nr * CAP] = jnp.zeros((BLK, BLK), BF)

    def help_on(a):
        for k in range(1, nr):
            src = lax.rem(r + nr - k, nr)
            ref = wb[a].at[pl.ds(CAP * src + per[a] * d, per[a])]
            drain(ref, whelp.at[a, k])
            for ky in range(1, nd):
                send(ref, ref, wsend.at[a], wrecv.at[a], ypeer(ky))

    sum_trees = {way: tree(n_of[way], n_of[way] // 2) for way in (1, -1)}

    weights_direct(1)
    publish()
    p_ref[...] = jnp.zeros_like(p_ref)
    a_ref[...] = jnp.zeros_like(a_ref)

    def tables():
        for k in range(1, nr):
            src = lax.rem(r + nr - k, nr)
            drain(meta_v.at[src], meta_r.at[k])
        to_smem = pltpu.make_async_copy(meta_v, meta_s, meta_l)
        to_smem.start()
        to_smem.wait()

    def weights_here(a):
        locals_[a].wait()
        got = (nr - 1) * DIRECT[a] + (nr - 1) * (nd - 1) * per[a]
        drain(wb[a].at[pl.ds(0, got)], wrecv.at[a])

    def forward(low, high):
        @pl.loop(low, high)
        def _(i):
            at = (i + 1) // 2
            where = lax.rem(z + nz + at * (1 - 2 * (i % 2)), nz)
            drain(xb.at[pl.ds(wide * where + third * (1 - h), third)], sib_r.at[i])
            owner = where // (KR // PB)
            base = (where % (KR // PB)) * PB
            left = xb[pl.ds(wide * where, wide)].reshape(wide * HALF, tokens).T
            right = jnp.concatenate(
                [
                    jnp.concatenate(
                        [wub[meta_s[owner, 6, (base + i) * NC + j]] for j in range(NC)], axis=1
                    )
                    for i in range(PB)
                ],
                axis=0,
            )
            p_ref[...] += jnp.dot(left, right, preferred_element_type=F32)

    longest = max(len(trees[way][0]) for way in (1, -1))
    for j in range(1, longest + 1):
        for a in range(2):
            for way in (1, -1):
                gather_step(a, way, j)
        for a in range(2):
            for way in (1, -1):
                gather_leaf(a, way, j)
        if j <= 2:
            help_on(j - 1)
    tables()
    weights_here(0)
    forward(0, nz)
    drain(xg[1].at[pl.ds(0, third * nz)], sib_all)

    step_rows = 4
    steps = nr * KR // step_rows
    per_owner = KR // step_rows
    deep = step_rows * BLK

    act, slope = gelu_parts(p_ref[...])
    act_low = act.astype(BF)
    for i in range(NC):
        act_t[i] = act_low[:, i * BLK:(i + 1) * BLK].T
        s_ref[pl.ds(i * BLK, BLK), :] = slope[:, i * BLK:(i + 1) * BLK].T

    def block_rows(ref, k):
        return jnp.concatenate([ref[2 * k], ref[2 * k + 1]], axis=0)

    ways = ((r, nr, xpeer), (d, nd, ypeer))
    share_y = CAP // nd
    part = share_y // 2

    def terms(a, e, k):
        place, count, _ = ways[e]
        first = lax.rem(place + k, count)

        @pl.loop(0, ways[1 - e][1])
        def _(second):
            owner, owner_y = (first, second) if e == 0 else (second, first)
            for u in range(part):
                s = share_y * owner_y + part * e + u
                if a == 0:
                    i, j = meta_s[owner, 3, s], meta_s[owner, 4, s]
                    keep = meta_s[owner, 5, s].astype(F32) * scale
                    term = nt_dot(act_t[i], block_rows(gb, j))
                else:
                    i, j = meta_s[owner, 0, s], meta_s[owner, 1, s]
                    keep = meta_s[owner, 2, s].astype(F32) * scale
                    term = nt_dot(block_rows(xb, i), pg_t[j])
                dw[a][e][k, second, u] = (term * keep).astype(BF)

    def halves(a, e, k, side):
        return dw[a][e].at[k, pl.ds(2 * side, 2)]

    def relay_out(a, e):
        for side, k in ((0, 1), (1, 3)):
            send(halves(a, e, 2, side), relay_in.at[a, e, side], one_s.at[a, e], relay_r.at[a, e, side], ways[e][2](k))

    def direct_out(a, e, k):
        side = 1 if k == 1 else 0
        send(halves(a, e, k, side), one_in.at[a, e, k // 2, side], one_s.at[a, e], one_r.at[a, e, k // 2, side], ways[e][2](k))

    def relay_on(a, e):
        for side, k in ((0, 1), (1, 3)):
            drain(relay_in.at[a, e, side], relay_r.at[a, e, side])

            @pl.loop(0, 2)
            def _(t):
                for u in range(part):
                    total = dw[a][e][k, 2 * side + t, u].astype(F32) + relay_in[a, e, side, t, u].astype(F32)
                    relayed[a, e, side, t, u] = total.astype(BF)

            send(
                relayed.at[a, e, side], one_in.at[a, e, k // 2, side], one_s.at[a, e],
                one_r.at[a, e, k // 2, side], ways[e][2](k),
            )

    def second_out(a, e):
        for k in range(2):
            for side in range(2):
                drain(one_in.at[a, e, k, side], one_r.at[a, e, k, side])

        @pl.loop(0, 2)
        def _(t):
            for side in range(2):
                for u in range(part):
                    total = dw[a][e][0, 2 * side + t, u].astype(F32)
                    for k in range(2):
                        total += one_in[a, e, k, side, t, u].astype(F32)
                    half_sum[a, e, 2 * side + t, u] = total.astype(BF)

        place, count, peer = ways[1 - e]
        for k in (2, 1, 3):
            to = lax.rem(place + k, count)
            send(half_sum.at[a, e, to], two_in.at[a, e, k - 1], two_s.at[a, e], two_r.at[a, e, k - 1], peer(k))

    def finish(a, e):
        place, count, _ = ways[1 - e]
        for k in range(count - 1):
            drain(two_in.at[a, e, k], two_r.at[a, e, k])
        out = (down_ref, up_ref)[a]
        for u in range(part):
            total = half_sum[a, e, place, u].astype(F32)
            for k in range(count - 1):
                total += two_in[a, e, k, u].astype(F32)
            out[0, 0, part * e + u] = total.astype(BF)

    def act_gradient():
        weights_here(1)

        @pl.loop(0, steps)
        def _(t):
            owner, base = t // per_owner, (t % per_owner) * step_rows
            right = gb[pl.ds(2 * step_rows * t, 2 * step_rows)].reshape(deep, tokens)
            left = jnp.concatenate(
                [
                    jnp.concatenate(
                        [wdb[meta_s[owner, 7, i * KR + base + j]] for j in range(step_rows)], axis=1
                    )
                    for i in range(NC)
                ],
                axis=0,
            )
            a_ref[...] += jnp.dot(left, right, preferred_element_type=F32)

        for i in range(NC):
            rows = pl.ds(i * BLK, BLK)
            pg_t[i] = (a_ref[rows, :] * s_ref[rows, :]).astype(BF)

    def partial_piece(index, k):
        where = lax.rem(z + nz + k, nz)
        owner = where // (KR // PB)
        base = (where % (KR // PB)) * PB
        left = jnp.concatenate(
            [
                jnp.concatenate(
                    [wub[meta_s[owner, 6, (base + i) * NC + j]] for j in range(NC)], axis=1
                )
                for i in range(PB)
            ],
            axis=0,
        )
        right = jnp.concatenate([pg_t[j] for j in range(NC)], axis=0)
        own[index] = jnp.dot(left, right, preferred_element_type=F32).reshape(2, width, tokens)
        mine[index] = own[index, 1 - h].astype(BF)
        send(mine.at[index], theirs.at[index], part_s, part_r.at[index], sibling)

    n_right, n_left = n_of[1], n_of[-1]

    def index_of(way, at):
        return at - 1 if way == 1 else n_right + at - 1

    order = []
    for at in range(n_right, 0, -1):
        order.append((1, at))
        if at <= n_left:
            order.append((-1, at))
    def summed(index, extra):
        drain(theirs.at[index], part_r.at[index])
        total = own[index, h] + theirs[index].astype(F32)
        for ref in extra:
            total = total + ref[...].astype(F32)
        return total

    def incoming(way, at):
        strides, marks = sum_trees[way]
        side = 0 if way == 1 else 1
        refs = []
        j = marks.index(at)
        if j < len(strides):
            if strides[j] == 2:
                refs.append((ring_leaf.at[side, at], leaf_r.at[side, at]))
            refs.append((ring_bone.at[side, at], bone_r.at[side, at]))
        return refs

    def ring_step(way, at):
        strides, marks = sum_trees[way]
        side = 0 if way == 1 else 1
        index = index_of(way, at)
        ref = ring_out.at[index]
        if at in marks:
            pairs = incoming(way, at)
            for more, sem in pairs:
                drain(more, sem)
            hop = strides[marks.index(at) - 1]
            ref[...] = summed(index, [more for more, _ in pairs]).astype(BF)
            send(ref, ring_bone.at[side, at - hop], ring_s, bone_r.at[side, at - hop], zpeer(way * hop))
        else:
            ref[...] = summed(index, []).astype(BF)
            send(ref, ring_leaf.at[side, at - 1], ring_s, leaf_r.at[side, at - 1], zpeer(way))

    def waits(way, at):
        return at in sum_trees[way][1][:-1]

    def ring_chain(level):
        for way in (1, -1):
            inner = sum_trees[way][1][1:-1][::-1]
            if level < len(inner):
                ring_step(way, inner[level])

    def ring_end():
        pairs = incoming(1, 0) + incoming(-1, 0)
        for ref, sem in pairs:
            drain(ref, sem)
        in_ref[...] = summed(nz - 1, [ref for ref, _ in pairs]).astype(BF)

    for e in (0, 1):
        terms(0, e, 2)
        relay_out(0, e)
    act_gradient()
    for e in (0, 1):
        terms(1, e, 2)
        relay_out(1, e)
    last = None
    for way, at in order:
        partial_piece(index_of(way, at), way * at)
        if last is not None and not waits(*last):
            ring_step(*last)
        last = (way, at)
    if not waits(*last):
        ring_step(*last)
    for a in (0, 1):
        for e in (0, 1):
            for k in (1, 3):
                terms(a, e, k)
                direct_out(a, e, k)
        if a == 0:
            ring_chain(0)
            for e in (0, 1):
                relay_on(a, e)
    ring_chain(1)
    partial_piece(nz - 1, 0)
    for e in (0, 1):
        relay_on(1, e)
    for a in (0, 1):
        for e in (0, 1):
            terms(a, e, 0)
    ring_chain(2)
    for e in (0, 1):
        second_out(0, e)
    ring_end()
    for e in (0, 1):
        second_out(1, e)
    for a in (0, 1):
        for e in (0, 1):
            finish(a, e)

    for a in range(2):
        drain(xg[a].at[pl.ds(0, third * (nz - 1))], ag_s.at[a])
        drain(xg[a].at[pl.ds(0, third * nz)], sib_s.at[a])
        gone = (nr - 1) * (per[a] + DIRECT[a]) + (nr - 1) * (nd - 1) * per[a]
        drain(wb[a].at[pl.ds(0, gone)], wsend.at[a])
    for k in range(1, nr):
        drain(meta_v.at[r], meta_ss.at[k])
    for a in range(2):
        for e in range(2):
            for _ in range(3):
                drain(relay_in.at[a, e], one_s.at[a, e])
            drain(two_in.at[a, e], two_s.at[a, e])

    drain(mine, part_s)
    drain(ring_out, ring_s)


def solution(mesh):
    nd, nr, nc = mesh.shape["dp"], mesh.shape["row"], mesh.shape["col"]
    nz = nc // 2
    DMA = pltpu.SemaphoreType.DMA
    VMEM = pltpu.VMEM

    def body(inputs, out_grad, up_blocks, up_index, down_blocks, down_index):
        tokens, width = inputs.shape
        blocks = nr * KR
        hidden = NC * BLK
        share = CAP // nd
        vmem = pl.BlockSpec(memory_space=pltpu.VMEM)
        smem = pl.BlockSpec(memory_space=pltpu.SMEM)
        hbm = pl.BlockSpec(memory_space=pltpu.HBM)
        scratch = [
            VMEM((blocks * BLK // HALF, HALF, tokens), BF),
            VMEM((blocks * BLK // HALF, HALF, tokens), BF),
            VMEM((nr * CAP + 1, BLK, BLK), BF),
            VMEM((nr * CAP + 1, BLK, BLK), BF),
            VMEM((nr, 8, BLK), jnp.int32),
            pltpu.SMEM((nr, 8, BLK), jnp.int32),
            VMEM((tokens, hidden), F32),
            VMEM((hidden, tokens), F32),
            VMEM((hidden, tokens), F32),
            VMEM((NC, BLK, tokens), BF),
            VMEM((NC, BLK, tokens), BF),
            VMEM((nr, nd, share // 2, BLK, BLK), BF),
            VMEM((nd, nr, share // 2, BLK, BLK), BF),
            VMEM((nr, nd, share // 2, BLK, BLK), BF),
            VMEM((nd, nr, share // 2, BLK, BLK), BF),
            VMEM((2, 2, 2, 2, share // 2, BLK, BLK), BF),
            VMEM((2, 2, 2, 2, share // 2, BLK, BLK), BF),
            VMEM((2, 2, 2, 2, 2, share // 2, BLK, BLK), BF),
            VMEM((2, 2, 4, share // 2, BLK, BLK), BF),
            VMEM((2, 2, 3, share // 2, BLK, BLK), BF),
            VMEM((nz, 2, width, tokens), F32),
            VMEM((nz, width, tokens), BF),
            VMEM((nz, width, tokens), BF),
            VMEM((nz - 1, width, tokens), BF),
            VMEM((2, nz // 2, width, tokens), BF),
            VMEM((2, nz // 2, width, tokens), BF),
            DMA((2,)),
            DMA((nr,)), DMA((nr,)), DMA,
            DMA((2,)), DMA((2, nr)), DMA((2,)), DMA((2,)),
            DMA((2,)), DMA((2, 2, nz // 2)),
            DMA((2,)), DMA((nz,)), DMA,
            DMA((2, 2)), DMA((2, 2, 2)), DMA((2, 2, 2, 2)),
            DMA((2, 2)), DMA((2, 2, 3)),
            DMA, DMA((nz,)),
            DMA, DMA((2, nz // 2)), DMA((2, nz // 2)),
        ]
        def units(array):
            return array.T.reshape(width // HALF, HALF, tokens)

        in_grad, up_grad, down_grad = pl.pallas_call(
            functools.partial(kernel, (nd, nr, nz)),
            out_shape=(
                jax.ShapeDtypeStruct((width, tokens), BF),
                jax.ShapeDtypeStruct((1, 1, share, BLK, BLK), BF),
                jax.ShapeDtypeStruct((1, 1, share, BLK, BLK), BF),
            ),
            in_specs=[hbm, hbm, hbm, smem, hbm, smem],
            out_specs=(vmem, vmem, vmem),
            scratch_shapes=scratch,
            compiler_params=pltpu.CompilerParams(
                collective_id=0, has_side_effects=True, vmem_limit_bytes=60 << 20
            ),
        )(units(inputs), units(out_grad), up_blocks, up_index, down_blocks, down_index)
        return in_grad.T, up_grad, down_grad

    return jax.shard_map(
        body,
        mesh=mesh,
        in_specs=(
            P(("dp", "row"), "col"),
            P(("dp", "row"), "col"),
            P("row", "col", None, None, None),
            P("row", "col", None),
            P("row", "col", None, None, None),
            P("row", "col", None),
        ),
        out_specs=(
            P(("dp", "row"), "col"),
            P("row", "col", "dp", None, None),
            P("row", "col", "dp", None, None),
        ),
        check_vma=False,
    )
```

time: 101 us -> 94.6 us (0.937)
  Pallas kernels: 94.7 us -> 90.1 us
  local copies, waits for them, and re-layouts: 5.68 us -> 3.68 us
    pallas_call x1, Pallas kernels: 94.7 us -> 90.1 us  [body(): pl.pallas_call(functools.partial(kernel, (nd, nr, nz)), out_shape=(jax.Sh...]
    unnamed x14 -> x5, local copies, waits for them, and re-layouts: 4.96 us -> 3.68 us
where the time goes in v2:
time: 94.6 us; the launch traced here: 94.4 us
  Pallas kernels  90.1 us (95%)
  local copies, waits for them, and re-layouts  3.68 us (4%)
    pallas_call x1, Pallas kernels, body(): pl.pallas_call(functools.partial(kernel, (nd, nr, nz)), out_shape=(jax.Sh...  90.1 us
    unnamed x5, local copies, waits for them, and re-layouts  3.68 us

profile of v2, /device:TPU:1, one launch (start us, length us, event | category | flops | bytes accessed | tf_op | source)
XLA Modules:
  0.0 94.4 jit_solution(1783560509530795115)
XLA Ops:
  0.6 90.1 %shard_map.85 = (bf16[192,128]{1,0:T(8,128)(2,1)}, bf16[1,1,4,128,128]{4,3,2,1,0:T(8,128)(2,1)}, bf16[1,1,4,128,128]{4,3,2,1,0:T(8,128)(2,1)}) custom-call(bf16[3,64,128]{2,1,0:T(8,128)(2,1)} %bitcast.8, bf16[3,64,128]{2,1,0:T(8,128)(2,1)} %bitcast.9, bf16[1,1,16,128,128]{4,3,2,1,0:T(8,128)(2,1)} %wu_hbm.1, s32[1,1,16]{2,1,0:T(1,128)} %ui_ref.1, ...), custom_call_target="tpu_custom_call" | custom-call | tf_op jit(solution)/shard_map/pallas_call | solution.py:569
  90.8 1.4 %copy.12 = bf16[128,192]{0,1:T(8,128)(2,1)} copy(bf16[128,192]{0,1:T(8,128)(2,1)} %bitcast.7) | data formatting | bytes 98304
  92.2 0.0 copy-start
  92.2 1.6 %copy.13 = bf16[1,1,4,128,128]{4,3,2,1,0:T(8,128)(2,1)} copy(bf16[1,1,4,128,128]{4,3,2,1,0:T(8,128)(2,1)} %get-tuple-element.13) | data formatting | bytes 262144
  93.8 0.0 copy-done
  93.8 0.7 copy.14
Async XLA Ops:
  92.2 1.6 %copy-start = (bf16[1,1,4,128,128]{4,3,2,1,0:T(8,128)(2,1)S(1)}, bf16[1,1,4,128,128]{4,3,2,1,0:T(8,128)(2,1)}, u32[]{:S(2)}) copy-start(bf16[1,1,4,128,128]{4,3,2,1,0:T(8,128)(2,1)} %get-tuple-element.14) | copy-start | bytes 393220

commit v3 on v2

--- a/solution.py
+++ b/solution.py
@@ -227,21 +227,20 @@
         got = (nr - 1) * DIRECT[a] + (nr - 1) * (nd - 1) * per[a]
         drain(wb[a].at[pl.ds(0, got)], wrecv.at[a])
 
-    def forward(low, high):
-        @pl.loop(low, high)
-        def _(i):
+    def forward():
+        for i in range(nz):
             at = (i + 1) // 2
             where = lax.rem(z + nz + at * (1 - 2 * (i % 2)), nz)
             drain(xb.at[pl.ds(wide * where + third * (1 - h), third)], sib_r.at[i])
-            owner = where // (KR // PB)
-            base = (where % (KR // PB)) * PB
-            left = xb[pl.ds(wide * where, wide)].reshape(wide * HALF, tokens).T
+
+        @pl.loop(0, nr)
+        def _(owner):
+            deep = KR * BLK
+            left = xb[pl.ds(2 * KR * owner, 2 * KR)].reshape(deep, tokens).T
             right = jnp.concatenate(
                 [
-                    jnp.concatenate(
-                        [wub[meta_s[owner, 6, (base + i) * NC + j]] for j in range(NC)], axis=1
-                    )
-                    for i in range(PB)
+                    jnp.concatenate([wub[meta_s[owner, 6, i * NC + j]] for j in range(NC)], axis=1)
+                    for i in range(KR)
                 ],
                 axis=0,
             )
@@ -259,10 +258,10 @@
             help_on(j - 1)
     tables()
     weights_here(0)
-    forward(0, nz)
+    forward()
     drain(xg[1].at[pl.ds(0, third * nz)], sib_all)
 
-    step_rows = 4
+    step_rows = 12
     steps = nr * KR // step_rows
     per_owner = KR // step_rows
     deep = step_rows * BLK
@@ -284,7 +283,7 @@
         place, count, _ = ways[e]
         first = lax.rem(place + k, count)
 
-        @pl.loop(0, ways[1 - e][1])
+        @pl.loop(0, ways[1 - e][1], unroll=2)
         def _(second):
             owner, owner_y = (first, second) if e == 0 else (second, first)
             for u in range(part):
@@ -378,6 +377,9 @@
             pg_t[i] = (a_ref[rows, :] * s_ref[rows, :]).astype(BF)
 
     def partial_piece(index, k):
+        partial_store(index, partial_dot(k))
+
+    def partial_dot(k):
         where = lax.rem(z + nz + k, nz)
         owner = where // (KR // PB)
         base = (where % (KR // PB)) * PB
@@ -391,7 +393,10 @@
             axis=0,
         )
         right = jnp.concatenate([pg_t[j] for j in range(NC)], axis=0)
-        own[index] = jnp.dot(left, right, preferred_element_type=F32).reshape(2, width, tokens)
+        return jnp.dot(left, right, preferred_element_type=F32)
+
+    def partial_store(index, both):
+        own[index] = both.reshape(2, width, tokens)
         mine[index] = own[index, 1 - h].astype(BF)
         send(mine.at[index], theirs.at[index], part_s, part_r.at[index], sibling)
 
@@ -461,14 +466,19 @@
     for e in (0, 1):
         terms(1, e, 2)
         relay_out(1, e)
-    last = None
-    for way, at in order:
-        partial_piece(index_of(way, at), way * at)
-        if last is not None and not waits(*last):
-            ring_step(*last)
-        last = (way, at)
-    if not waits(*last):
-        ring_step(*last)
+    before = []
+    for at in range(n_right, 0, -1):
+        both = [(way, at) for way in (1, -1) if at <= n_of[way]]
+        dots = [partial_dot(way * at) for way, at in both]
+        for (way, at), value in zip(both, dots):
+            partial_store(index_of(way, at), value)
+        for one in before:
+            if not waits(*one):
+                ring_step(*one)
+        before = both
+    for one in before:
+        if not waits(*one):
+            ring_step(*one)
     for a in (0, 1):
         for e in (0, 1):
             for k in (1, 3):

time: 94.6 us -> 84.2 us (0.89)
  the two profiles are of different devices: /device:TPU:1 before, /device:TPU:32 now
where the time goes in v3:
time: 84.2 us; the launch traced here: 84 us
  Pallas kernels  79.7 us (95%)
  local copies, waits for them, and re-layouts  3.68 us (4%)
    pallas_call x1, Pallas kernels, body(): pl.pallas_call(functools.partial(kernel, (nd, nr, nz)), out_shape=(jax.Sh...  79.7 us
    unnamed x5, local copies, waits for them, and re-layouts  3.68 us

profile of v3, /device:TPU:32, one launch (start us, length us, event | category | flops | bytes accessed | tf_op | source)
XLA Modules:
  0.0 84.0 jit_solution(15240660125546314851)
XLA Ops:
  0.6 79.7 %shard_map.85 = (bf16[192,128]{1,0:T(8,128)(2,1)}, bf16[1,1,4,128,128]{4,3,2,1,0:T(8,128)(2,1)}, bf16[1,1,4,128,128]{4,3,2,1,0:T(8,128)(2,1)}) custom-call(bf16[3,64,128]{2,1,0:T(8,128)(2,1)} %bitcast.8, bf16[3,64,128]{2,1,0:T(8,128)(2,1)} %bitcast.9, bf16[1,1,16,128,128]{4,3,2,1,0:T(8,128)(2,1)} %wu_hbm.1, s32[1,1,16]{2,1,0:T(1,128)} %ui_ref.1, ...), custom_call_target="tpu_custom_call" | custom-call | tf_op jit(solution)/shard_map/pallas_call | solution.py:579
  80.3 1.4 %copy.12 = bf16[128,192]{0,1:T(8,128)(2,1)} copy(bf16[128,192]{0,1:T(8,128)(2,1)} %bitcast.7) | data formatting | bytes 98304
  81.8 0.0 copy-start
  81.8 1.6 %copy.13 = bf16[1,1,4,128,128]{4,3,2,1,0:T(8,128)(2,1)} copy(bf16[1,1,4,128,128]{4,3,2,1,0:T(8,128)(2,1)} %get-tuple-element.13) | data formatting | bytes 262144
  83.4 0.0 copy-done
  83.4 0.7 copy.14
Async XLA Ops:
  81.8 1.6 %copy-start = (bf16[1,1,4,128,128]{4,3,2,1,0:T(8,128)(2,1)S(1)}, bf16[1,1,4,128,128]{4,3,2,1,0:T(8,128)(2,1)}, u32[]{:S(2)}) copy-start(bf16[1,1,4,128,128]{4,3,2,1,0:T(8,128)(2,1)} %get-tuple-element.14) | copy-start | bytes 393220

commit v4 on v3

--- a/solution.py
+++ b/solution.py
@@ -283,7 +283,7 @@
         place, count, _ = ways[e]
         first = lax.rem(place + k, count)
 
-        @pl.loop(0, ways[1 - e][1], unroll=2)
+        @pl.loop(0, ways[1 - e][1], unroll=4)
         def _(second):
             owner, owner_y = (first, second) if e == 0 else (second, first)
             for u in range(part):

time: 84.2 us -> 83 us (0.986)
  Pallas kernels: 79.7 us -> 78.5 us
    pallas_call x1, Pallas kernels: 79.7 us -> 78.5 us  [body(): pl.pallas_call(functools.partial(kernel, (nd, nr, nz)), out_shape=(jax.Sh...]
where the time goes in v4:
time: 83 us; the launch traced here: 82.8 us
  Pallas kernels  78.5 us (95%)
  local copies, waits for them, and re-layouts  3.68 us (4%)
    pallas_call x1, Pallas kernels, body(): pl.pallas_call(functools.partial(kernel, (nd, nr, nz)), out_shape=(jax.Sh...  78.5 us
    unnamed x5, local copies, waits for them, and re-layouts  3.68 us

profile of v4, /device:TPU:32, one launch (start us, length us, event | category | flops | bytes accessed | tf_op | source)
XLA Modules:
  0.0 82.8 jit_solution(4654270477972020519)
XLA Ops:
  0.6 78.5 %shard_map.85 = (bf16[192,128]{1,0:T(8,128)(2,1)}, bf16[1,1,4,128,128]{4,3,2,1,0:T(8,128)(2,1)}, bf16[1,1,4,128,128]{4,3,2,1,0:T(8,128)(2,1)}) custom-call(bf16[3,64,128]{2,1,0:T(8,128)(2,1)} %bitcast.8, bf16[3,64,128]{2,1,0:T(8,128)(2,1)} %bitcast.9, bf16[1,1,16,128,128]{4,3,2,1,0:T(8,128)(2,1)} %wu_hbm.1, s32[1,1,16]{2,1,0:T(1,128)} %ui_ref.1, ...), custom_call_target="tpu_custom_call" | custom-call | tf_op jit(solution)/shard_map/pallas_call | solution.py:579
  79.2 1.4 %copy.12 = bf16[128,192]{0,1:T(8,128)(2,1)} copy(bf16[128,192]{0,1:T(8,128)(2,1)} %bitcast.7) | data formatting | bytes 98304
  80.6 0.0 copy-start
  80.6 1.6 %copy.13 = bf16[1,1,4,128,128]{4,3,2,1,0:T(8,128)(2,1)} copy(bf16[1,1,4,128,128]{4,3,2,1,0:T(8,128)(2,1)} %get-tuple-element.13) | data formatting | bytes 262144
  82.2 0.0 copy-done
  82.2 0.7 copy.14
Async XLA Ops:
  80.6 1.6 %copy-start = (bf16[1,1,4,128,128]{4,3,2,1,0:T(8,128)(2,1)S(1)}, bf16[1,1,4,128,128]{4,3,2,1,0:T(8,128)(2,1)}, u32[]{:S(2)}) copy-start(bf16[1,1,4,128,128]{4,3,2,1,0:T(8,128)(2,1)} %get-tuple-element.14) | copy-start | bytes 393220
